TPU v7x, 32 devices: a whole 2x2x4 slice. The times are simulated.
32 devices in a mesh: ctx: 8 (over y, x, core), head: 4 (over z).
Axes of the slice: x: 2, y: 2, z: 4, core: 2. Of those that a mesh axis runs over, the one named last changes fastest.
Arguments:
- queries: bfloat16 [2048, 4096], P('ctx', 'head'), may hold values from -5 to 5
- keys: bfloat16 [2048, 4096], P('ctx', 'head'), may hold values from -5 to 5
- values: bfloat16 [2048, 4096], P('ctx', 'head'), may hold values from -1300 to 1300
- gate_logits: bfloat16 [2048, 4096], P('ctx', 'head'), may hold values from -6 to 6
- norm_gain: float32 [4096], replicated, may hold values from 0.1 to 1.9
- out_weight: bfloat16 [4096, 6144], P(None, 'head'), may hold values from -0.09375 to 0.09375
- residual: bfloat16 [2048, 6144], P('ctx', 'head'), may hold values from -4 to 4
Outputs:
- layer_out: bfloat16 [2048, 6144], P('ctx', 'head')
All inputs are finite; a program needn't handle non-finite values.
Results may differ from a plain program's by a relative error of at most 0.011.
Values may be sent and summed in bfloat16 or wider, within the bound.
A program may use at most 64 MiB of HBM per device.

v0:
```python
import jax
import jax.numpy as jnp
from jax import lax
from jax.sharding import PartitionSpec as P

HEAD_DIM = 128
BLOCK = 256
INNER = 4096


epsilon = 1e-06


def prefix(shard, axis, join, neutral):
    place = lax.axis_index(axis)
    gathered = lax.all_gather(shard.astype(jnp.bfloat16), axis)
    state = jnp.zeros_like(shard) + jnp.asarray(neutral, shard.dtype)

    def one(hop, state):
        return join(state, lax.dynamic_index_in_dim(gathered, hop, 0, False).astype(shard.dtype))

    return lax.fori_loop(0, place, one, state)


def add_states(earlier, later):
    return earlier + later


def on_device(queries, keys, values, gate_logits, norm_gain, out_weight, residual):
    tok_rows, feature_width = queries.shape
    heads_here = feature_width // HEAD_DIM
    block_count = tok_rows // BLOCK

    def head_columns(array, head_number):
        columns = array[:, head_number * HEAD_DIM : (head_number + 1) * HEAD_DIM]
        return columns.reshape(block_count, BLOCK, HEAD_DIM)

    state_list = []
    for head_number in range(heads_here):
        key_head = head_columns(keys, head_number)
        value_head = head_columns(values, head_number)
        state_list.append(
            jnp.einsum("bsd,bse->bde", key_head, value_head, preferred_element_type=jnp.float32)
        )
    block_state = jnp.stack(state_list, axis=1)
    own_state = jnp.sum(block_state, axis=0)
    earlier_state = prefix(own_state, "ctx", add_states, jnp.zeros_like(own_state))
    prefix_state = earlier_state[None] + (jnp.cumsum(block_state, axis=0) - block_state)
    state_high = prefix_state.astype(jnp.bfloat16)
    state_low = (prefix_state - state_high.astype(jnp.float32)).astype(jnp.bfloat16)
    causal_mask = jnp.tril(jnp.ones((BLOCK, BLOCK), dtype=bool))
    head_outputs = []
    for head_number in range(heads_here):
        query_head = head_columns(queries, head_number)
        key_head = head_columns(keys, head_number)
        value_head = head_columns(values, head_number)
        scores = jnp.einsum(
            "btd,bsd->bts", query_head, key_head, preferred_element_type=jnp.float32
        )
        scores = jnp.where(causal_mask[None], scores, jnp.float32(0.0)).astype(jnp.bfloat16)
        local_part = jnp.einsum(
            "bts,bsd->btd", scores, value_head, preferred_element_type=jnp.float32
        )
        carried_part = jnp.einsum(
            "btd,bde->bte",
            query_head,
            state_high[:, head_number],
            preferred_element_type=jnp.float32,
        )
        carried_part = carried_part + jnp.einsum(
            "btd,bde->bte",
            query_head,
            state_low[:, head_number],
            preferred_element_type=jnp.float32,
        )
        head_outputs.append((local_part + carried_part).reshape(tok_rows, HEAD_DIM))
    attended = jnp.concatenate(head_outputs, axis=1).astype(jnp.bfloat16)
    attended_float = attended.astype(jnp.float32)
    square_total = lax.psum(jnp.sum(attended_float * attended_float, axis=1), "head")
    scale_rows = lax.rsqrt(square_total / INNER + epsilon)
    gain_here = lax.dynamic_slice_in_dim(
        norm_gain, lax.axis_index("head") * feature_width, feature_width, 0
    )
    normed = (
        attended_float
        * scale_rows[:, None]
        * gain_here[None, :]
        * jax.nn.sigmoid(gate_logits.astype(jnp.float32))
    )
    normed = normed.astype(jnp.bfloat16)
    projected = jnp.dot(
        lax.all_gather(normed, "head", axis=1, tiled=True),
        out_weight,
        preferred_element_type=jnp.float32,
    )
    return (projected + residual.astype(jnp.float32)).astype(jnp.bfloat16)


def solution(mesh):
    in_specs = (
        P("ctx", "head"),
        P("ctx", "head"),
        P("ctx", "head"),
        P("ctx", "head"),
        P(),
        P(None, "head"),
        P("ctx", "head"),
    )
    out_specs = P("ctx", "head")
    return jax.shard_map(
        on_device, mesh=mesh, in_specs=in_specs, out_specs=out_specs, check_vma=False
    )
```

profile of v0, /device:TPU:0, one launch (start us, length us, event | category | flops | bytes accessed | tf_op | source)
XLA Modules:
  0.0 135.7 jit_solution(4287403144237155106)
XLA Ops:
  6.5 1.1 constant_dynamic-update-slice_fusion.7
  7.7 1.1 constant_dynamic-update-slice_fusion.6
  8.8 1.1 constant_dynamic-update-slice_fusion.5
  9.8 1.1 constant_dynamic-update-slice_fusion.4
  10.9 1.1 constant_dynamic-update-slice_fusion.3
  12.0 1.1 constant_dynamic-update-slice_fusion.2
  13.1 1.1 constant_dynamic-update-slice_fusion.1
  14.2 1.1 constant_dynamic-update-slice_fusion
  15.3 0.0 copy-start.5
  15.3 0.7 copy-done.5
  16.0 0.0 all-gather.3.cloned.1.call-update
  16.0 0.0 all-gather.5.cloned.1.call-start
  16.0 0.2 copy.9
  16.4 30.4 %all-gather.3.cloned.1.call-done = bf16[8,8,128,128]{3,2,1,0:T(8,128)(2,1)} async-done(((bf16[1,8,128,128]{3,2,1,0:T(8,128)(2,1)}), bf16[8,8,128,128]{3,2,1,0:T(8,128)(2,1)}) %all-gather.3.cloned.1.call-update) | async-done | bytes 2097168 | tf_op jit(solution)/shard_map/all_gather | solution.py:16
  46.8 0.0 copy-start
  46.8 0.1 fusion.53
  46.9 0.9 copy-done
  47.8 0.2 fusion.113
  48.0 0.2 fusion.118
  48.2 0.2 fusion.123
  48.4 0.2 fusion.128
  48.6 0.2 fusion.133
  48.8 0.2 fusion.138
  49.0 0.2 fusion.143
  49.2 0.2 fusion.148
  49.4 0.2 fusion.25
  49.6 0.9 fusion.26
  50.5 0.9 fusion.27
  51.4 0.2 fusion.28
  51.5 0.2 fusion.29
  51.7 0.2 fusion.30
  51.9 0.2 fusion.31
  52.1 0.2 fusion.32
  52.4 0.4 fusion.34
  52.7 0.0 dynamic-slice-start
  52.8 0.4 fusion.36
  53.1 0.4 fusion.38
  53.5 0.4 fusion.40
  53.9 0.4 fusion.42
  54.3 1.3 fusion.44
  55.6 1.3 fusion.46
  56.9 0.4 fusion.48
  57.2 0.2 fusion.49
  57.4 11.7 %psum.7 = f32[256]{0:T(256)S(1)} all-reduce(f32[256]{0:T(256)S(1)} %fusion.49), channel_id=1, replica_groups=mesh['ctx'=8,'head'=4] {'head'}, use_global_device_ids=true, to_apply=%region_3.4 | all-reduce | flops 256 | bytes 2048 | tf_op jit(solution)/shard_map/psum | solution.py:79
  69.1 1.1 fusion.52
  70.3 0.0 all-gather.5.cloned.1.call-update
  70.3 49.1 %all-gather.5.cloned.1.call-done = bf16[256,4096]{0,1:T(8,128)(2,1)} async-done(((bf16[256,1024]{0,1:T(8,128)(2,1)}), bf16[256,4096]{0,1:T(8,128)(2,1)}) %all-gather.5.cloned.1.call-update) | async-done | bytes 2097168 | tf_op jit(solution)/shard_map/all_gather | solution.py:92
  119.4 9.5 %fusion = bf16[256,1536]{1,0:T(8,128)(2,1)} fusion(bf16[256,4096]{0,1:T(8,128)(2,1)} %all-gather.5.cloned.1.call-done, bf16[4096,1536]{1,0:T(8,128)(2,1)} %param.14, bf16[256,1536]{1,0:T(8,128)(2,1)S(1)} %copy-done.1), kind=kOutput, calls=%fused_computation.2 | convolution fusion | flops 3222405120 | bytes 16252928 | tf_op jit(solution)/shard_map/dot_general | solution.py:91
  (21 shorter events, 0.1 us)
Async XLA Ops:
  6.5 9.5 %copy-start.4 = (bf16[256,1024]{1,0:T(8,128)(2,1)S(1)}, bf16[256,1024]{1,0:T(8,128)(2,1)}, u32[]{:S(2)}) copy-start(bf16[256,1024]{1,0:T(8,128)(2,1)} %param.12) | copy-start | bytes 1572868
  6.5 40.2 %all-gather.3.cloned.1.call-start = ((), (), s32[]{:S(2)}) async-start(), calls=%async_computation | async-start | bytes 2359296 | tf_op jit(solution)/shard_map/all_gather | solution.py:16
  15.3 0.7 copy-start.5
  16.0 103.4 %all-gather.5.cloned.1.call-start = ((), (), s32[]{:S(2)}) async-start(), calls=%async_computation.1 | async-start | bytes 2621440 | tf_op jit(solution)/shard_map/all_gather | solution.py:92
  46.8 1.0 copy-start
  48.2 4.1 %copy-start.2 = (bf16[256,1024]{1,0:T(8,128)(2,1)S(1)}, bf16[256,1024]{1,0:T(8,128)(2,1)}, u32[]{:S(2)}) copy-start(bf16[256,1024]{1,0:T(8,128)(2,1)} %param.11) | copy-start | bytes 1572868
  48.2 4.1 %copy-start.3 = (bf16[256,1024]{1,0:T(8,128)(2,1)S(1)}, bf16[256,1024]{1,0:T(8,128)(2,1)}, u32[]{:S(2)}) copy-start(bf16[256,1024]{1,0:T(8,128)(2,1)} %param.10) | copy-start | bytes 1572868
  52.7 16.4 %dynamic-slice-start = ((f32[4096]{0:T(1024)}, s32[]{:T(128)}), f32[1024]{0:T(1024)S(1)}, s32[]{:S(2)}) async-start(f32[4096]{0:T(1024)} %param.13, s32[]{:T(128)} %select_n.50), calls=%async_computation.2 | async-start | bytes 8704 | tf_op jit(solution)/shard_map/dynamic_slice | solution.py:81
  54.2 65.1 %copy-start.1 = (bf16[256,1536]{1,0:T(8,128)(2,1)S(1)}, bf16[256,1536]{1,0:T(8,128)(2,1)}, u32[]{:S(2)}) copy-start(bf16[256,1536]{1,0:T(8,128)(2,1)} %param.15) | copy-start | bytes 2359300
Sparse Core Ops, SparseCore 0:
  16.1 30.5 all-gather.2
  70.4 48.9 all-gather.4
where the time goes:
time: 136 us
  waiting for transfers between devices  79.5 us (58%)
  matrix products  27.5 us (20%)
  between operations  13.7 us (10%)
  blocking collectives  11.7 us (9%)
  local copies, waits for them, and re-layouts  1.91 us (1%)
  other arithmetic  1.44 us (1%)
    all_gather x1, waiting for transfers between devices, on_device(): lax.all_gather(normed, 'head', axis=1, tiled=True)  49.1 us
    all_gather x1, waiting for transfers between devices, prefix(): gathered = lax.all_gather(shard.astype(jnp.bfloat16), axis)  30.4 us
    psum x1, blocking collectives, on_device(): lax.psum(jnp.sum(attended_float * attended_float, axis=1), 'head')  11.7 us
    dot_general x1, matrix products, on_device(): jnp.dot(lax.all_gather(normed, 'head', axis=1, tiled=True), out_weight, p...  9.52 us
    dot_general x8, matrix products, on_device(): jnp.einsum('bsd,bse->bde', key_head, value_head, preferred_element_type=j...  8.67 us
    dot_general x8, matrix products, on_device(): jnp.einsum('bts,bsd->btd', scores, value_head, preferred_element_type=jnp...  4.8 us
    dot_general x8, matrix products, on_device(): jnp.einsum('btd,bde->bte', query_head, state_low[:, head_number], preferr...  2.93 us
  transfers between devices with their start and end apart: 2, of which 2 were waited for; matrix products, arithmetic and copies ran while one was open for 0% of the time, Pallas kernels for 0%

commit v1 on v0

v1 whole, which is shorter than its diff:
```python
import functools

import jax
import jax.numpy as jnp
from jax import lax
from jax.experimental import pallas as pl
from jax.experimental.pallas import tpu as pltpu
from jax.sharding import PartitionSpec as P

HEAD_DIM = 128
EPSILON = 1e-06
MESH = pl.DeviceIdType.MESH
F32 = jnp.float32
BF16 = jnp.bfloat16


def kernel(
    steps, n_head, group,
    q_hbm, k_hbm, v_hbm, gate_hbm, gain_ref, w_hbm, res_hbm, out_ref,
    qb, kb, vb, gb, rb, wb, yall, acc, loc, tot, pre, st_send, st_recv, sq, ms,
    in_sem, w_sem, st_ssem, st_rsem, z_ssem, z_rsem, ms_ssem, ms_rsem,
):
    rows, width = qb.shape
    heads = width // HEAD_DIM
    groups = heads // group
    group_width = group * HEAD_DIM
    out_width = out_ref.shape[1]
    me_c = lax.axis_index("ctx")
    me_h = lax.axis_index("head")

    loads = [
        pltpu.make_async_copy(source, target, in_sem.at[number])
        for number, (source, target) in enumerate(
            ((k_hbm, kb), (v_hbm, vb), (q_hbm, qb), (gate_hbm, gb), (res_hbm, rb))
        )
    ]
    w_loads = [
        pltpu.make_async_copy(
            w_hbm.at[pl.ds(o * width, width)], wb.at[pl.ds(o * width, width)], w_sem.at[o]
        )
        for o in range(n_head)
    ]
    for load in loads:
        load.start()

    def bit(step):
        return lax.rem(me_c // (2**step), 2)

    def partner(step):
        return me_c + (2**step) * (1 - 2 * bit(step))

    barrier = pltpu.get_barrier_semaphore()
    for step in range(steps):
        pl.semaphore_signal(
            barrier, inc=1, device_id={"ctx": partner(step)}, device_id_type=MESH
        )
    for d in range(1, n_head):
        pl.semaphore_signal(
            barrier, inc=1, device_id={"head": lax.rem(me_h + d, n_head)}, device_id_type=MESH
        )

    def state_rows(g):
        return pl.ds(g * group_width, group_width)

    def state_copy(step, g):
        return pltpu.make_async_remote_copy(
            src_ref=st_send.at[step, state_rows(g)],
            dst_ref=st_recv.at[step, state_rows(g)],
            send_sem=st_ssem.at[step, g],
            recv_sem=st_rsem.at[step, g],
            device_id={"ctx": partner(step)},
            device_id_type=MESH,
        )

    def send_state(step, g):
        st_send[step, state_rows(g), :] = tot[state_rows(g), :].astype(BF16)
        state_copy(step, g).start()

    def head_cols(h):
        return pl.ds(h * HEAD_DIM, HEAD_DIM)

    loads[0].wait()
    loads[1].wait()
    for load in w_loads:
        load.start()

    def own_state(g):
        for h in range(g * group, (g + 1) * group):
            tot[head_cols(h), :] = lax.dot_general(
                kb[:, head_cols(h)], vb[:, head_cols(h)], (((0,), (0,)), ((), ())),
                preferred_element_type=F32,
            )

    own_state(0)
    pl.semaphore_wait(barrier, steps + n_head - 1)
    for g in range(groups):
        if g > 0:
            own_state(g)
        send_state(0, g)
    pre[...] = jnp.zeros_like(pre)
    sq[...] = jnp.zeros_like(sq)
    loads[2].wait()
    loads[3].wait()

    def local(g):
        at = lax.broadcasted_iota(jnp.int32, (rows, rows), 0)
        of = lax.broadcasted_iota(jnp.int32, (rows, rows), 1)
        for h in range(g * group, (g + 1) * group):
            scores = lax.dot_general(
                qb[:, head_cols(h)], kb[:, head_cols(h)], (((1,), (1,)), ((), ())),
                preferred_element_type=F32,
            )
            scores = jnp.where(of <= at, scores, 0.0).astype(BF16)
            loc[:, head_cols(h)] = jnp.dot(
                scores, vb[:, head_cols(h)], preferred_element_type=F32
            )

    def z_copy(way, hop, c, origin):
        return pltpu.make_async_remote_copy(
            src_ref=yall.at[origin, c],
            dst_ref=yall.at[origin, c],
            send_sem=z_ssem.at[way, hop - 1, c],
            recv_sem=z_rsem.at[way, hop - 1, c],
            device_id={"head": me_h + 1 - 2 * way},
            device_id_type=MESH,
        )

    def finish(g):
        for number in range(group):
            h = g * group + number
            carried = jnp.dot(
                qb[:, head_cols(h)], pre[head_cols(h), :].astype(BF16),
                preferred_element_type=F32,
            )
            attended = (loc[:, head_cols(h)] + carried).astype(BF16).astype(F32)
            sq[...] += attended * attended
            gain = gain_ref[:, pl.ds(pl.multiple_of(me_h * width + h * HEAD_DIM, HEAD_DIM), HEAD_DIM)]
            gate = gb[:, head_cols(h)].astype(F32)
            yall[me_h, g, :, head_cols(number)] = (
                attended * gain * (1.0 / (1.0 + jnp.exp(-gate)))
            ).astype(BF16)

        @pl.when(me_h < n_head - 1)
        def _():
            z_copy(0, 1, g, me_h).start()

        @pl.when(me_h > 0)
        def _():
            z_copy(1, 1, g, me_h).start()

    for wave in range(max(groups, groups + steps - 1)):
        if wave < groups:
            local(wave)
        for step in reversed(range(steps)):
            g = wave - step
            if not 0 <= g < groups:
                continue
            state_copy(step, g).wait_recv()
            got = st_recv[step, state_rows(g), :].astype(F32)
            if step < steps - 1:
                tot[state_rows(g), :] += got
                send_state(step + 1, g)
            pre[state_rows(g), :] += jnp.where(bit(step) == 1, got, 0.0)
            if step == steps - 1:
                finish(g)
        if steps == 0:
            finish(wave)

    def ms_copy(d, source):
        return pltpu.make_async_remote_copy(
            src_ref=ms.at[source],
            dst_ref=ms.at[source],
            send_sem=ms_ssem.at[d],
            recv_sem=ms_rsem.at[d],
            device_id={"head": lax.rem(me_h + d, n_head)},
            device_id_type=MESH,
        )

    row_total = jnp.sum(jnp.transpose(sq[...]), axis=0, keepdims=True)
    ms[me_h] = jnp.broadcast_to(row_total, ms.shape[1:])
    for d in range(1, n_head):
        ms_copy(d, me_h).start()
    acc[...] = jnp.zeros_like(acc)
    loads[4].wait()
    for load in w_loads:
        load.wait()

    def project(origin, c):
        at = pl.multiple_of(origin * width + c * group_width, group_width)
        acc[...] += jnp.dot(
            yall[origin, c], wb[pl.ds(at, group_width), :], preferred_element_type=F32
        )

    for d in range(1, n_head):
        def arrive(c, carry, d=d):
            @pl.when(me_h - d >= 0)
            def _():
                z_copy(0, d, c, me_h - d).wait_recv()

                @pl.when(me_h < n_head - 1)
                def _():
                    z_copy(0, d + 1, c, me_h - d).start()

            @pl.when(me_h + d < n_head)
            def _():
                z_copy(1, d, c, me_h + d).wait_recv()

                @pl.when(me_h > 0)
                def _():
                    z_copy(1, d + 1, c, me_h + d).start()

            if d == 1:
                project(me_h, c)

            @pl.when(me_h - d >= 0)
            def _():
                project(me_h - d, c)

            @pl.when(me_h + d < n_head)
            def _():
                project(me_h + d, c)

            return carry

        lax.fori_loop(0, groups, arrive, 0)

    for d in range(1, n_head):
        ms_copy(d, lax.rem(me_h + n_head - d, n_head)).wait_recv()
    total = ms[0, 0:1, :]
    for o in range(1, n_head):
        total = total + ms[o, 0:1, :]
    scale = lax.rsqrt(total / (n_head * width) + EPSILON)
    scale = jnp.transpose(jnp.broadcast_to(scale, (HEAD_DIM, rows)))
    for j in range(out_width // HEAD_DIM):
        out_ref[:, head_cols(j)] = (
            acc[:, head_cols(j)] * scale + rb[:, head_cols(j)].astype(F32)
        ).astype(out_ref.dtype)

    for step in range(steps):
        for g in range(groups):
            state_copy(step, g).wait_send()
    for d in range(1, n_head):
        ms_copy(d, me_h).wait_send()
        for c in range(groups):
            @pl.when(jnp.logical_and(me_h < n_head - 1, me_h - (d - 1) >= 0))
            def _(c=c, d=d):
                z_copy(0, d, c, me_h - (d - 1)).wait_send()

            @pl.when(jnp.logical_and(me_h > 0, me_h + (d - 1) < n_head))
            def _(c=c, d=d):
                z_copy(1, d, c, me_h + (d - 1)).wait_send()


def solution(mesh):
    n_ctx, n_head = mesh.shape["ctx"], mesh.shape["head"]
    steps = n_ctx.bit_length() - 1
    assert n_ctx == 2**steps

    def on_device(queries, keys, values, gate_logits, norm_gain, out_weight, residual):
        rows, width = queries.shape
        inner, out_width = out_weight.shape
        heads = width // HEAD_DIM
        group = 2 if heads % 2 == 0 else 1
        groups = heads // group
        group_width = group * HEAD_DIM
        anywhere = pl.BlockSpec(memory_space=pl.ANY)
        vmem = pl.BlockSpec(memory_space=pltpu.VMEM)
        dma = pltpu.SemaphoreType.DMA
        hops = max(n_head - 1, 1)
        stages = max(steps, 1)
        return pl.pallas_call(
            functools.partial(kernel, steps, n_head, group),
            out_shape=jax.ShapeDtypeStruct((rows, out_width), residual.dtype),
            in_specs=[anywhere] * 4 + [vmem] + [anywhere] * 2,
            out_specs=vmem,
            scratch_shapes=[
                pltpu.VMEM((rows, width), BF16),
                pltpu.VMEM((rows, width), BF16),
                pltpu.VMEM((rows, width), BF16),
                pltpu.VMEM((rows, width), BF16),
                pltpu.VMEM((rows, out_width), BF16),
                pltpu.VMEM((inner, out_width), BF16),
                pltpu.VMEM((n_head, groups, rows, group_width), BF16),
                pltpu.VMEM((rows, out_width), F32),
                pltpu.VMEM((rows, width), F32),
                pltpu.VMEM((width, HEAD_DIM), F32),
                pltpu.VMEM((width, HEAD_DIM), F32),
                pltpu.VMEM((stages, width, HEAD_DIM), BF16),
                pltpu.VMEM((stages, width, HEAD_DIM), BF16),
                pltpu.VMEM((rows, HEAD_DIM), F32),
                pltpu.VMEM((n_head, 8, rows), F32),
                dma((5,)),
                dma((n_head,)),
                dma((stages, groups)),
                dma((stages, groups)),
                dma((2, hops, groups)),
                dma((2, hops, groups)),
                dma((n_head,)),
                dma((n_head,)),
            ],
            compiler_params=pltpu.CompilerParams(
                collective_id=0, has_side_effects=True, vmem_limit_bytes=48 * 1024 * 1024
            ),
        )(queries, keys, values, gate_logits, norm_gain[None, :], out_weight, residual)

    in_specs = (
        P("ctx", "head"),
        P("ctx", "head"),
        P("ctx", "head"),
        P("ctx", "head"),
        P(),
        P(None, "head"),
        P("ctx", "head"),
    )
    return jax.shard_map(
        on_device, mesh=mesh, in_specs=in_specs, out_specs=P("ctx", "head"), check_vma=False
    )
```

time: 136 us -> 59.1 us (0.43)
  waiting for transfers between devices: 79.5 us -> 0 us
  Pallas kernels: 0 us -> 51.8 us
  matrix products: 27.5 us -> 0 us
  between operations: 13.7 us -> 0.02 us
  blocking collectives: 11.7 us -> 0 us
  local copies, waits for them, and re-layouts: 1.91 us -> 6.9 us
  other arithmetic: 1.44 us -> 0 us
    all_gather x2 -> x0, waiting for transfers between devices: 79.4 us -> none  [the longest x1 49.1 us: on_device(): lax.all_gather(normed, 'head', axis=1, tiled=True)]
    pallas_call x0 -> x1, Pallas kernels: none -> 51.8 us  [on_device(): pl.pallas_call(functools.partial(kernel, steps, n_head, group), out_shape...]
    dot_general x33 -> x0, matrix products: 27.5 us -> none  [the longest x1 9.52 us: on_device(): jnp.dot(lax.all_gather(normed, 'head', axis=1, tiled=True), out_weight, p...]
    psum x1 -> x0, blocking collectives: 11.7 us -> none  [on_device(): lax.psum(jnp.sum(attended_float * attended_float, axis=1), 'head')]
    unnamed x20 -> x13, local copies, waits for them, and re-layouts: 1.86 us -> 6.9 us
  transfers between devices with their start and end apart: 2 -> 0, of which waited for: 2 -> 0; matrix products, arithmetic and copies ran while one was open for 0% -> 0% of each run, Pallas kernels for 0% -> 0%
where the time goes in v1:
time: 59.1 us; the launch traced here: 58.7 us
  Pallas kernels  51.8 us (88%)
  local copies, waits for them, and re-layouts  6.9 us (12%)
    pallas_call x1, Pallas kernels, on_device(): pl.pallas_call(functools.partial(kernel, steps, n_head, group), out_shape...  51.8 us
    unnamed x13, local copies, waits for them, and re-layouts  6.9 us

profile of v1, /device:TPU:0, one launch (start us, length us, event | category | flops | bytes accessed | tf_op | source)
XLA Modules:
  0.0 58.7 jit_solution(863739824583468266)
XLA Ops:
  0.0 0.0 copy-start
  0.0 1.1 %copy-done = bf16[256,1536]{1,0:T(8,128)(2,1)S(1)} copy-done((bf16[256,1536]{1,0:T(8,128)(2,1)S(1)}, bf16[256,1536]{1,0:T(8,128)(2,1)}, u32[]{:S(2)}) %copy-start) | copy-done | bytes 786456
  1.1 0.0 copy-start.1
  1.1 1.0 %copy-done.1 = bf16[256,1024]{1,0:T(8,128)(2,1)S(1)} copy-done((bf16[256,1024]{1,0:T(8,128)(2,1)S(1)}, bf16[256,1024]{1,0:T(8,128)(2,1)}, u32[]{:S(2)}) %copy-start.1) | copy-done | bytes 524312
  2.2 0.0 copy-start.2
  2.2 1.0 %copy-done.2 = bf16[256,1024]{1,0:T(8,128)(2,1)S(1)} copy-done((bf16[256,1024]{1,0:T(8,128)(2,1)S(1)}, bf16[256,1024]{1,0:T(8,128)(2,1)}, u32[]{:S(2)}) %copy-start.2) | copy-done | bytes 524312
  3.2 0.0 copy-start.3
  3.2 1.0 %copy-done.3 = bf16[256,1024]{1,0:T(8,128)(2,1)S(1)} copy-done((bf16[256,1024]{1,0:T(8,128)(2,1)S(1)}, bf16[256,1024]{1,0:T(8,128)(2,1)}, u32[]{:S(2)}) %copy-start.3) | copy-done | bytes 524312
  4.3 0.0 copy-start.4
  4.3 1.0 %copy-done.4 = bf16[256,1024]{1,0:T(8,128)(2,1)S(1)} copy-done((bf16[256,1024]{1,0:T(8,128)(2,1)S(1)}, bf16[256,1024]{1,0:T(8,128)(2,1)}, u32[]{:S(2)}) %copy-start.4) | copy-done | bytes 524312
  5.3 0.0 copy-start.5
  5.3 0.7 %copy-done.5 = f32[4096]{0:T(1024)S(1)} copy-done((f32[4096]{0:T(1024)S(1)}, f32[4096]{0:T(1024)}, u32[]{:S(2)}) %copy-start.5) | copy-done | bytes 16408
  6.0 51.8 %shard_map.73 = bf16[256,1536]{1,0:T(8,128)(2,1)S(1)} custom-call(bf16[256,1024]{1,0:T(8,128)(2,1)S(1)} %copy-done.1, bf16[256,1024]{1,0:T(8,128)(2,1)S(1)} %copy-done.2, bf16[256,1024]{1,0:T(8,128)(2,1)S(1)} %copy-done.3, bf16[256,1024]{1,0:T(8,128)(2,1)S(1)} %copy-done.4, f32[1,4096]{1,0:T(1,128)S(1)} %bitcast.1, bf16[4096,1536]{1,0:T(8,128)(2,1)} %w_hbm.1, ...), custom_call_target="tpu_custom_call" | custom-call | tf_op jit(solution)/shard_map/pallas_call | solution.py:271
  57.8 0.9 %copy.9 = bf16[256,1536]{1,0:T(8,128)(2,1)} copy(bf16[256,1536]{1,0:T(8,128)(2,1)S(1)} %shard_map.73) | data formatting | bytes 1572864
Async XLA Ops:
  0.0 1.1 %copy-start = (bf16[256,1536]{1,0:T(8,128)(2,1)S(1)}, bf16[256,1536]{1,0:T(8,128)(2,1)}, u32[]{:S(2)}) copy-start(bf16[256,1536]{1,0:T(8,128)(2,1)} %res_hbm.1) | copy-start | bytes 2359300
  1.1 1.0 %copy-start.1 = (bf16[256,1024]{1,0:T(8,128)(2,1)S(1)}, bf16[256,1024]{1,0:T(8,128)(2,1)}, u32[]{:S(2)}) copy-start(bf16[256,1024]{1,0:T(8,128)(2,1)} %q_hbm.1) | copy-start | bytes 1572868
  2.2 1.0 %copy-start.2 = (bf16[256,1024]{1,0:T(8,128)(2,1)S(1)}, bf16[256,1024]{1,0:T(8,128)(2,1)}, u32[]{:S(2)}) copy-start(bf16[256,1024]{1,0:T(8,128)(2,1)} %k_hbm.1) | copy-start | bytes 1572868
  3.2 1.0 %copy-start.3 = (bf16[256,1024]{1,0:T(8,128)(2,1)S(1)}, bf16[256,1024]{1,0:T(8,128)(2,1)}, u32[]{:S(2)}) copy-start(bf16[256,1024]{1,0:T(8,128)(2,1)} %v_hbm.1) | copy-start | bytes 1572868
  4.3 1.0 %copy-start.4 = (bf16[256,1024]{1,0:T(8,128)(2,1)S(1)}, bf16[256,1024]{1,0:T(8,128)(2,1)}, u32[]{:S(2)}) copy-start(bf16[256,1024]{1,0:T(8,128)(2,1)} %gate_hbm.1) | copy-start | bytes 1572868
  5.3 0.7 %copy-start.5 = (f32[4096]{0:T(1024)S(1)}, f32[4096]{0:T(1024)}, u32[]{:S(2)}) copy-start(f32[4096]{0:T(1024)} %param.11) | copy-start | bytes 49156

commit v2 on v1

--- a/solution.py
+++ b/solution.py
@@ -299,7 +299,7 @@
                 dma((n_head,)),
             ],
             compiler_params=pltpu.CompilerParams(
-                collective_id=0, has_side_effects=True, vmem_limit_bytes=48 * 1024 * 1024
+                collective_id=0, has_side_effects=True, vmem_limit_bytes=62 * 1024 * 1024
             ),
         )(queries, keys, values, gate_logits, norm_gain[None, :], out_weight, residual)
 

time: 59.1 us -> 55.5 us (0.939)
  local copies, waits for them, and re-layouts: 6.9 us -> 2.06 us
  Pallas kernels: 51.8 us -> 53.2 us
    unnamed x13 -> x1, local copies, waits for them, and re-layouts: 6.9 us -> 2.06 us
    pallas_call x1, Pallas kernels: 51.8 us -> 53.2 us  [on_device(): pl.pallas_call(functools.partial(kernel, steps, n_head, group), out_shape...]
where the time goes in v2:
time: 55.5 us; the launch traced here: 55.3 us
  Pallas kernels  53.2 us (96%)
  local copies, waits for them, and re-layouts  2.06 us (4%)
    pallas_call x1, Pallas kernels, on_device(): pl.pallas_call(functools.partial(kernel, steps, n_head, group), out_shape...  53.2 us
    unnamed x1, local copies, waits for them, and re-layouts  2.06 us

profile of v2, /device:TPU:0, one launch (start us, length us, event | category | flops | bytes accessed | tf_op | source)
XLA Modules:
  0.0 55.3 jit_solution(14277123411860208309)
XLA Ops:
  0.0 53.2 %shard_map.73 = bf16[256,1536]{1,0:T(8,128)(2,1)} custom-call(bf16[256,1024]{1,0:T(8,128)(2,1)} %q_hbm.1, bf16[256,1024]{1,0:T(8,128)(2,1)} %k_hbm.1, bf16[256,1024]{1,0:T(8,128)(2,1)} %v_hbm.1, bf16[256,1024]{1,0:T(8,128)(2,1)} %gate_hbm.1, f32[1,4096]{1,0:T(1,128)} %bitcast.1, bf16[4096,1536]{1,0:T(8,128)(2,1)} %w_hbm.1, bf16[256,1536]{1,0:T(8,128)(2,1)} %res_hbm.1), custom_call_target="tpu_custom_call" | custom-call | tf_op jit(solution)/shard_map/pallas_call | solution.py:271
  53.2 2.1 %copy.9 = bf16[256,1536]{1,0:T(8,128)(2,1)} copy(bf16[256,1536]{1,0:T(8,128)(2,1)} %shard_map.73) | data formatting | bytes 1572864

commit v3 on v2

--- a/solution.py
+++ b/solution.py
@@ -15,7 +15,7 @@
 
 
 def kernel(
-    steps, n_head, group,
+    stages, n_head, group,
     q_hbm, k_hbm, v_hbm, gate_hbm, gain_ref, w_hbm, res_hbm, out_ref,
     qb, kb, vb, gb, rb, wb, yall, acc, loc, tot, pre, st_send, st_recv, sq, ms,
     in_sem, w_sem, st_ssem, st_rsem, z_ssem, z_rsem, ms_ssem, ms_rsem,
@@ -43,17 +43,27 @@
     for load in loads:
         load.start()
 
-    def bit(step):
-        return lax.rem(me_c // (2**step), 2)
-
-    def partner(step):
-        return me_c + (2**step) * (1 - 2 * bit(step))
+    slots, last = [], len(stages) - 1
+    for stage, (weight, radix) in enumerate(stages):
+        slots.append([])
+        for m in range(1, radix):
+            slots[stage].append((sum(map(len, slots)), m))
+
+    def digit(stage):
+        weight, radix = stages[stage]
+        return lax.rem(me_c // weight, radix)
+
+    def partner(stage, m):
+        weight, radix = stages[stage]
+        own = digit(stage)
+        return me_c + weight * (lax.rem(own + m, radix) - own)
 
     barrier = pltpu.get_barrier_semaphore()
-    for step in range(steps):
-        pl.semaphore_signal(
-            barrier, inc=1, device_id={"ctx": partner(step)}, device_id_type=MESH
-        )
+    for stage in range(len(stages)):
+        for _, m in slots[stage]:
+            pl.semaphore_signal(
+                barrier, inc=1, device_id={"ctx": partner(stage, m)}, device_id_type=MESH
+            )
     for d in range(1, n_head):
         pl.semaphore_signal(
             barrier, inc=1, device_id={"head": lax.rem(me_h + d, n_head)}, device_id_type=MESH
@@ -62,19 +72,44 @@
     def state_rows(g):
         return pl.ds(g * group_width, group_width)
 
-    def state_copy(step, g):
+    def state_copy(stage, slot, m, g):
         return pltpu.make_async_remote_copy(
-            src_ref=st_send.at[step, state_rows(g)],
-            dst_ref=st_recv.at[step, state_rows(g)],
-            send_sem=st_ssem.at[step, g],
-            recv_sem=st_rsem.at[step, g],
-            device_id={"ctx": partner(step)},
+            src_ref=st_send.at[stage, state_rows(g)],
+            dst_ref=st_recv.at[slot, state_rows(g)],
+            send_sem=st_ssem.at[slot, g],
+            recv_sem=st_rsem.at[slot, g],
+            device_id={"ctx": partner(stage, m)},
             device_id_type=MESH,
         )
 
-    def send_state(step, g):
-        st_send[step, state_rows(g), :] = tot[state_rows(g), :].astype(BF16)
-        state_copy(step, g).start()
+    def to_later(stage, m, act):
+        if stage < last:
+            act()
+        else:
+            pl.when(digit(stage) + m < stages[stage][1])(act)
+
+    def from_earlier(stage, m, act):
+        if stage < last:
+            act()
+        else:
+            pl.when(digit(stage) - m >= 0)(act)
+
+    def send_state(stage, g):
+        st_send[stage, state_rows(g), :] = tot[state_rows(g), :].astype(BF16)
+        for slot, m in slots[stage]:
+            to_later(stage, m, lambda: state_copy(stage, slot, m, g).start())
+
+    def take_state(stage, g):
+        for slot, m in slots[stage]:
+            def take():
+                state_copy(stage, slot, m, g).wait_recv()
+                got = st_recv[slot, state_rows(g), :].astype(F32)
+                if stage < last:
+                    tot[state_rows(g), :] += got
+                    got = jnp.where(digit(stage) >= m, got, 0.0)
+                pre[state_rows(g), :] += got
+
+            from_earlier(stage, m, take)
 
     def head_cols(h):
         return pl.ds(h * HEAD_DIM, HEAD_DIM)
@@ -92,11 +127,12 @@
             )
 
     own_state(0)
-    pl.semaphore_wait(barrier, steps + n_head - 1)
+    pl.semaphore_wait(barrier, sum(map(len, slots)) + n_head - 1)
     for g in range(groups):
         if g > 0:
             own_state(g)
-        send_state(0, g)
+        if stages:
+            send_state(0, g)
     pre[...] = jnp.zeros_like(pre)
     sq[...] = jnp.zeros_like(sq)
     loads[2].wait()
@@ -148,23 +184,16 @@
         def _():
             z_copy(1, 1, g, me_h).start()
 
-    for wave in range(max(groups, groups + steps - 1)):
-        if wave < groups:
-            local(wave)
-        for step in reversed(range(steps)):
-            g = wave - step
-            if not 0 <= g < groups:
-                continue
-            state_copy(step, g).wait_recv()
-            got = st_recv[step, state_rows(g), :].astype(F32)
-            if step < steps - 1:
-                tot[state_rows(g), :] += got
-                send_state(step + 1, g)
-            pre[state_rows(g), :] += jnp.where(bit(step) == 1, got, 0.0)
-            if step == steps - 1:
-                finish(g)
-        if steps == 0:
-            finish(wave)
+    for stage in range(last):
+        for g in range(groups):
+            take_state(stage, g)
+            send_state(stage + 1, g)
+    for g in range(groups):
+        local(g)
+    for g in range(groups):
+        if stages:
+            take_state(last, g)
+        finish(g)
 
     def ms_copy(d, source):
         return pltpu.make_async_remote_copy(
@@ -236,9 +265,10 @@
             acc[:, head_cols(j)] * scale + rb[:, head_cols(j)].astype(F32)
         ).astype(out_ref.dtype)
 
-    for step in range(steps):
-        for g in range(groups):
-            state_copy(step, g).wait_send()
+    for stage in range(len(stages)):
+        for slot, m in slots[stage]:
+            for g in range(groups):
+                to_later(stage, m, lambda: state_copy(stage, slot, m, g).wait_send())
     for d in range(1, n_head):
         ms_copy(d, me_h).wait_send()
         for c in range(groups):
@@ -255,6 +285,9 @@
     n_ctx, n_head = mesh.shape["ctx"], mesh.shape["head"]
     steps = n_ctx.bit_length() - 1
     assert n_ctx == 2**steps
+    stages = [(1, 2)] if steps % 2 else []
+    for bit in range(steps % 2, steps, 2):
+        stages.append((2**bit, 4))
 
     def on_device(queries, keys, values, gate_logits, norm_gain, out_weight, residual):
         rows, width = queries.shape
@@ -267,9 +300,10 @@
         vmem = pl.BlockSpec(memory_space=pltpu.VMEM)
         dma = pltpu.SemaphoreType.DMA
         hops = max(n_head - 1, 1)
-        stages = max(steps, 1)
+        stage_count = max(len(stages), 1)
+        slot_count = max(sum(radix - 1 for _, radix in stages), 1)
         return pl.pallas_call(
-            functools.partial(kernel, steps, n_head, group),
+            functools.partial(kernel, tuple(stages), n_head, group),
             out_shape=jax.ShapeDtypeStruct((rows, out_width), residual.dtype),
             in_specs=[anywhere] * 4 + [vmem] + [anywhere] * 2,
             out_specs=vmem,
@@ -285,14 +319,14 @@
                 pltpu.VMEM((rows, width), F32),
                 pltpu.VMEM((width, HEAD_DIM), F32),
                 pltpu.VMEM((width, HEAD_DIM), F32),
-                pltpu.VMEM((stages, width, HEAD_DIM), BF16),
-                pltpu.VMEM((stages, width, HEAD_DIM), BF16),
+                pltpu.VMEM((stage_count, width, HEAD_DIM), BF16),
+                pltpu.VMEM((slot_count, width, HEAD_DIM), BF16),
                 pltpu.VMEM((rows, HEAD_DIM), F32),
                 pltpu.VMEM((n_head, 8, rows), F32),
                 dma((5,)),
                 dma((n_head,)),
-                dma((stages, groups)),
-                dma((stages, groups)),
+                dma((slot_count, groups)),
+                dma((slot_count, groups)),
                 dma((2, hops, groups)),
                 dma((2, hops, groups)),
                 dma((n_head,)),

time: 55.5 us -> 54.6 us (0.984)
  the two profiles are of different devices: /device:TPU:0 before, /device:TPU:4 now
where the time goes in v3:
time: 54.6 us; the launch traced here: 54.3 us
  Pallas kernels  52.2 us (96%)
  local copies, waits for them, and re-layouts  2.06 us (4%)
    pallas_call x1, Pallas kernels, on_device(): pl.pallas_call(functools.partial(kernel, tuple(stages), n_head, group), o...  52.2 us
    unnamed x1, local copies, waits for them, and re-layouts  2.06 us

profile of v3, /device:TPU:4, one launch (start us, length us, event | category | flops | bytes accessed | tf_op | source)
XLA Modules:
  0.0 54.3 jit_solution(13834114962678453078)
XLA Ops:
  0.0 52.2 %shard_map.73 = bf16[256,1536]{1,0:T(8,128)(2,1)} custom-call(bf16[256,1024]{1,0:T(8,128)(2,1)} %q_hbm.1, bf16[256,1024]{1,0:T(8,128)(2,1)} %k_hbm.1, bf16[256,1024]{1,0:T(8,128)(2,1)} %v_hbm.1, bf16[256,1024]{1,0:T(8,128)(2,1)} %gate_hbm.1, f32[1,4096]{1,0:T(1,128)} %bitcast.1, bf16[4096,1536]{1,0:T(8,128)(2,1)} %w_hbm.1, bf16[256,1536]{1,0:T(8,128)(2,1)} %res_hbm.1), custom_call_target="tpu_custom_call" | custom-call | tf_op jit(solution)/shard_map/pallas_call | solution.py:305
  52.3 2.1 %copy.9 = bf16[256,1536]{1,0:T(8,128)(2,1)} copy(bf16[256,1536]{1,0:T(8,128)(2,1)} %shard_map.73) | data formatting | bytes 1572864

commit v4 on v3

--- a/solution.py
+++ b/solution.py
@@ -116,8 +116,6 @@
 
     loads[0].wait()
     loads[1].wait()
-    for load in w_loads:
-        load.start()
 
     def own_state(g):
         for h in range(g * group, (g + 1) * group):
@@ -188,6 +186,8 @@
         for g in range(groups):
             take_state(stage, g)
             send_state(stage + 1, g)
+    for load in w_loads:
+        load.start()
     for g in range(groups):
         local(g)
     for g in range(groups):

time: 54.6 us -> 54.6 us (level)
  no operation moved by 1% of the time
where the time goes in v4:
time: 54.6 us; the launch traced here: 54.3 us
  Pallas kernels  52.2 us (96%)
  local copies, waits for them, and re-layouts  2.06 us (4%)
    pallas_call x1, Pallas kernels, on_device(): pl.pallas_call(functools.partial(kernel, tuple(stages), n_head, group), o...  52.2 us
    unnamed x1, local copies, waits for them, and re-layouts  2.06 us

profile of v4, /device:TPU:4, one launch (start us, length us, event | category | flops | bytes accessed | tf_op | source)
XLA Modules:
  0.0 54.3 jit_solution(4800890940873862711)
XLA Ops:
  0.0 52.2 %shard_map.73 = bf16[256,1536]{1,0:T(8,128)(2,1)} custom-call(bf16[256,1024]{1,0:T(8,128)(2,1)} %q_hbm.1, bf16[256,1024]{1,0:T(8,128)(2,1)} %k_hbm.1, bf16[256,1024]{1,0:T(8,128)(2,1)} %v_hbm.1, bf16[256,1024]{1,0:T(8,128)(2,1)} %gate_hbm.1, f32[1,4096]{1,0:T(1,128)} %bitcast.1, bf16[4096,1536]{1,0:T(8,128)(2,1)} %w_hbm.1, bf16[256,1536]{1,0:T(8,128)(2,1)} %res_hbm.1), custom_call_target="tpu_custom_call" | custom-call | tf_op jit(solution)/shard_map/pallas_call | solution.py:305
  52.3 2.1 %copy.9 = bf16[256,1536]{1,0:T(8,128)(2,1)} copy(bf16[256,1536]{1,0:T(8,128)(2,1)} %shard_map.73) | data formatting | bytes 1572864
